TPU v7x, 128 devices: a whole 4x4x4 slice. The times are simulated.
128 devices in a mesh: block: 4 (over x), span: 8 (over z, core), stream: 4 (over y).
Axes of the slice: x: 4, y: 4, z: 4, core: 2. Of those that a mesh axis runs over, the one named last changes fastest.
Arguments:
- flow_state: float32 [4, 256, 16, 5, 4096], P('block', 'stream', None, None, 'span'), may hold values from -6 to 6
- wave_speed: float32 [4, 256, 16, 4096], P('block', 'stream', None, 'span'), may hold values from 0.5 to 2
- char_scale: float32 [5], replicated, may hold values from 0.002 to 4
- span_ratio: float32 [5], replicated, may hold values from 0.3 to 1
- send_tile: int32 [4, 8, 4, 32, 16], P('block', 'span', 'stream'), may hold values from 0 to 1023
- recv_tile: int32 [4, 8, 4, 32, 16], P('block', 'span', 'stream'), may hold values from 0 to 1023, as said below
- recv_live: int32 [4, 8, 4, 32, 16], P('block', 'span', 'stream'), may hold values from 0 to 1, as said below
- interp_weight: float32 [4, 8, 4, 32, 16], P('block', 'span', 'stream'), may hold values from 0.2 to 1
Outputs:
- new_state: float32 [4, 256, 16, 5, 4096], P('block', 'stream', None, None, 'span')
Inputs may be any that keep to these rules, and one draw needn't show every extreme that they name: `recv_tile`: the 512 entries of one device are all different. `recv_live`: on each device the live slots from one peer come first; every device has 16 live slots from at least one peer, and one device has 16 from every peer.
All inputs are finite; a program needn't handle non-finite values.
Results may differ from a plain program's by a relative error of at most 0.000088.
Values sent between devices are 32-bit elements; how exact they have to be, the bound alone decides.
A program may use at most 256 MiB of HBM per device.

v0:
```python
import jax
import jax.numpy as jnp
from jax import lax
from jax.sharding import PartitionSpec as P


def extended(block, sides, width):
    for axis, dim in sides:
        count = lax.axis_size(axis)
        forward = [(i, i + 1) for i in range(count - 1)]
        backward = [(target, source) for source, target in forward]
        low = lax.ppermute(
            lax.slice_in_dim(block, block.shape[dim] - width, None, axis=dim), axis, forward
        )
        high = lax.ppermute(lax.slice_in_dim(block, 0, width, axis=dim), axis, backward)
        block = jnp.concatenate([low, block, high], axis=dim)
    return block


def from_behind(block, axis, distance):
    devices = range(lax.axis_size(axis))
    route = [(i - distance, i) for i in devices if i - distance in devices]
    return lax.ppermute(block, axis, route)


def minmod(first_diff, second_diff):
    return jnp.maximum(jnp.minimum(first_diff, second_diff), 0.0) + jnp.minimum(
        jnp.maximum(first_diff, second_diff), 0.0
    )


def face_value(behind, centre, forward):
    return centre + 0.5 * minmod(centre - behind, forward - centre)


def on_device(
    flow_state, wave_speed, char_scale, span_ratio, send_tile, recv_tile, recv_live, interp_weight
):
    peer_count = lax.axis_size("block") * lax.axis_size("span")
    blocks_here, width_x, rows_y, components, width_z = flow_state.shape
    capacity = send_tile.shape[-1]
    tile_count = width_x * rows_y
    tile_rows = flow_state.reshape(tile_count, components * width_z)
    outgoing = tile_rows[send_tile.reshape(-1)]
    direct = outgoing.reshape(peer_count, capacity, components, width_z)
    arrived = lax.all_to_all(direct, ("block", "span"), split_axis=0, concat_axis=0, tiled=True)
    arrived = arrived.reshape(peer_count * capacity, components * width_z)
    targets = recv_tile.reshape(-1)
    previous = tile_rows[targets]
    scaled = (interp_weight.reshape(-1) * recv_live.reshape(-1).astype(jnp.float32))[:, None]
    delta = scaled * (arrived - previous)
    placement = (targets[:, None] == jnp.arange(tile_count, dtype=jnp.int32)[None, :]).astype(
        jnp.float32
    )
    added = lax.dot_general(
        placement,
        delta,
        (((0,), (0,)), ((), ())),
        precision=lax.Precision.HIGHEST,
        preferred_element_type=jnp.float32,
    )
    filled = (tile_rows + added).reshape(flow_state.shape)
    edge_cells = jnp.concatenate([filled[..., :2], filled[..., width_z - 2 :]], axis=4)
    edge_speed = jnp.concatenate([wave_speed[..., :2], wave_speed[..., width_z - 2 :]], axis=3)[
        :, :, :, None, :
    ]
    edge_stack = jnp.concatenate([edge_cells, edge_speed], axis=3)
    span_ext = extended(edge_stack, (("span", 4),), 2)
    low_cols = span_ext[:, :, :, :components, :2]
    high_cols = span_ext[:, :, :, :components, 6:8]
    row_cells = jnp.concatenate([filled[:, :2], filled[:, width_x - 2 :]], axis=1)
    row_speed = jnp.concatenate([wave_speed[:, :2], wave_speed[:, width_x - 2 :]], axis=1)[
        :, :, :, None, :
    ]
    row_stack = jnp.concatenate([row_cells, row_speed], axis=3)
    stream_ext = extended(row_stack, (("stream", 1),), 2)
    before_cells = stream_ext[:, :2, :, :components]
    before_speed = stream_ext[:, 1:2, :, components]
    after_cells = stream_ext[:, 6:7, :, :components]
    rate_x = char_scale[:, None]
    rate_z = (char_scale * span_ratio)[:, None]
    here_speed = wave_speed[:, :, :, None, :]
    prior_speed = jnp.concatenate([before_speed, wave_speed[:, : width_x - 1]], axis=1)[
        :, :, :, None, :
    ]
    stream_wide = jnp.concatenate([before_cells, filled, after_cells], axis=1)
    right_x = (
        rate_x
        * here_speed
        * face_value(
            stream_wide[:, 1 : width_x + 1],
            stream_wide[:, 2 : width_x + 2],
            stream_wide[:, 3 : width_x + 3],
        )
    )
    left_x = (
        rate_x
        * prior_speed
        * face_value(
            stream_wide[:, 0:width_x],
            stream_wide[:, 1 : width_x + 1],
            stream_wide[:, 2 : width_x + 2],
        )
    )
    face_before = face_value(low_cols[..., 0:1], low_cols[..., 1:2], filled[..., 0:1])
    face_first = face_value(low_cols[..., 1:2], filled[..., 0:1], filled[..., 1:2])
    face_inner = face_value(
        filled[..., : width_z - 2], filled[..., 1 : width_z - 1], filled[..., 2:]
    )
    face_last = face_value(
        filled[..., width_z - 2 : width_z - 1], filled[..., width_z - 1 :], high_cols[..., 0:1]
    )
    left_z = rate_z * jnp.concatenate([face_before, face_first, face_inner], axis=4)
    right_z = rate_z * jnp.concatenate([face_first, face_inner, face_last], axis=4)
    residual = left_x - right_x + left_z - right_z
    courant = 100.0 * rate_x * here_speed
    courant_prior = 100.0 * rate_x * prior_speed
    coupling = courant_prior / (1.0 + courant)
    source = 100.0 * residual / (1.0 + courant)
    line_shape = (blocks_here, rows_y, components, width_z)

    def advance(index, carry):
        growth_all, local_all, run_growth, run_local = carry
        factor = lax.dynamic_index_in_dim(coupling, index, 1, keepdims=False)
        term = lax.dynamic_index_in_dim(source, index, 1, keepdims=False)
        run_growth = factor * run_growth
        run_local = factor * run_local + term
        growth_all = lax.dynamic_update_index_in_dim(growth_all, run_growth, index, 1)
        local_all = lax.dynamic_update_index_in_dim(local_all, run_local, index, 1)
        return (growth_all, local_all, run_growth, run_local)

    start = (
        jnp.zeros_like(coupling),
        jnp.zeros_like(source),
        jnp.ones(line_shape, jnp.float32),
        jnp.zeros(line_shape, jnp.float32),
    )
    growth, local_part, last_growth, last_local = lax.fori_loop(0, width_x, advance, start)
    inflow = jnp.zeros_like(last_local)
    for relay_turn in range(lax.axis_size("stream") - 1):
        outflow = last_growth * inflow + last_local
        inflow = from_behind(outflow, "stream", 1)
    return filled + local_part + growth * inflow[:, None]


def solution(mesh):
    return jax.shard_map(
        on_device,
        mesh=mesh,
        in_specs=(
            P("block", "stream", None, None, "span"),
            P("block", "stream", None, "span"),
            P(),
            P(),
            P("block", "span", "stream", None, None),
            P("block", "span", "stream", None, None),
            P("block", "span", "stream", None, None),
            P("block", "span", "stream", None, None),
        ),
        out_specs=P("block", "stream", None, None, "span"),
        check_vma=False,
    )
```

profile of v0, /device:TPU:80, one launch (start us, length us, event | category | flops | bytes accessed | tf_op | source)
XLA Modules:
  0.0 543.2 jit_solution(5175209106161243631)
XLA Ops:
  0.9 20.5 %copy.47 = f32[1,64,16,5,512]{4,3,2,1,0:T(8,128)} copy(f32[1,64,16,5,512]{4,2,3,1,0:T(8,128)} %param.10) | data formatting | bytes 20971520 | tf_op args[0]
  21.4 20.5 %copy.78 = f32[128,8,5,512]{3,1,2,0:T(8,128)} copy(f32[128,8,5,512]{3,2,1,0:T(8,128)} %bitcast.46) | data formatting | bytes 20971520
  41.9 10.6 %gather_fusion = f32[512,2560]{1,0:T(8,128)} fusion(f32[1024,2560]{1,0:T(8,128)} %bitcast.43, s32[1024]{0:T(1024)S(1)} %pad_clamp_fusion.1), kind=kCustom, calls=%fused_computation | custom fusion | bytes 10487808 | tf_op jit(solution)/shard_map/gather | solution.py:44
  52.4 8.3 %reshape.215 = f32[32,16,5,512]{3,2,1,0:T(8,128)} reshape(f32[512,2560]{1,0:T(8,128)} %gather_fusion) | data formatting | bytes 10485760 | tf_op jit(solution)/shard_map/reshape | solution.py:45
  60.8 10.5 %copy.51 = f32[32,16,5,512]{3,1,2,0:T(8,128)} copy(f32[32,16,5,512]{3,2,1,0:T(8,128)} %reshape.215) | data formatting | bytes 10485760 | tf_op jit(solution)/shard_map/reshape | solution.py:45
  71.3 7.6 %all-to-all-start = ((f32[32,16,5,512]{3,1,2,0:T(8,128)}), f32[32,16,5,512]{3,1,2,0:T(8,128)}, u32[]{:S(2)}, u32[]{:S(2)}) async-start(f32[32,16,5,512]{3,1,2,0:T(8,128)} %copy.51), calls=%async_computation | async-start | bytes 10485760 | tf_op jit(solution)/shard_map/all_to_all | solution.py:46
  79.4 3.2 slice.104
  85.6 10.7 %gather_fusion.1 = f32[512,2560]{1,0:T(8,128)} fusion(f32[1024,2560]{1,0:T(8,128)} %bitcast.44, s32[1024]{0:T(1024)S(1)} %pad_clamp_fusion), kind=kCustom, calls=%fused_computation.1 | custom fusion | bytes 10487808 | tf_op jit(solution)/shard_map/gather | solution.py:49
  96.5 43.3 %all-to-all-done = f32[32,16,5,512]{3,1,2,0:T(8,128)} async-done(((f32[32,16,5,512]{3,1,2,0:T(8,128)}), f32[32,16,5,512]{3,1,2,0:T(8,128)}, u32[]{:S(2)}, u32[]{:S(2)}) %all-to-all-start) | async-done | bytes 5242912 | tf_op jit(solution)/shard_map/all_to_all | solution.py:46
  139.8 6.9 %copy.52 = f32[32,16,5,512]{3,2,1,0:T(8,128)S(1)} copy(f32[32,16,5,512]{3,1,2,0:T(8,128)} %all-to-all-done) | data formatting | bytes 10485760 | tf_op jit(solution)/shard_map/all_to_all | solution.py:46
  146.7 5.1 copy.79
  151.9 14.8 %convolution_add_fusion = f32[1024,2560]{1,0:T(8,128)} fusion(f32[1024,2560]{1,0:T(8,128)} %bitcast.45, f32[512,2560]{1,0:T(8,128)S(1)} %bitcast.50, f32[512,2560]{1,0:T(8,128)S(1)} %bitcast.49, f32[512]{0:T(512)S(1)} %mul.207, s32[512]{0:T(512)S(1)} %eq.15), kind=kOutput, calls=%fused_computation.28 | convolution fusion | flops 16111894528 | bytes 31461376 | tf_op jit(solution)/shard_map/dot_general | solution.py:55
  166.7 15.7 %reshape.218 = f32[1,64,16,5,512]{4,3,2,1,0:T(8,128)} reshape(f32[1024,2560]{1,0:T(8,128)} %convolution_add_fusion) | data formatting | bytes 20971520 | tf_op jit(solution)/shard_map/reshape | solution.py:62
  183.8 9.0 %fusion.14 = (f32[1,64,16,5,2]{4,3,2,1,0:T(8,128)}, f32[1,64,16,5,2]{4,3,2,1,0:T(8,128)}) fusion(f32[1,64,16,5,512]{4,3,2,1,0:T(8,128)} %reshape.218), kind=kLoop, calls=%fused_computation.55 | loop fusion | bytes 163840 | tf_op jit(solution)/shard_map/slice | solution.py:63
  192.8 10.9 %multiply_add_fusion.1 = f32[1,64,16,5,510]{4,3,2,1,0:T(8,128)} fusion(f32[1,64,16,5,512]{4,3,2,1,0:T(8,128)S(1)} %copy-done), kind=kLoop, calls=%fused_computation.23 | loop fusion | flops 23500800 | bytes 41779200 | tf_op jit(solution)/shard_map/add | solution.py:33
  203.7 7.7 %fusion.13 = (f32[1,64,16,5,1]{4,3,2,1,0:T(8,128)}, f32[1,64,16,5,1]{4,3,2,1,0:T(8,128)}, f32[1,64,16,5,1]{4,3,2,1,0:T(8,128)}, f32[1,64,16,5,1]{4,3,2,1,0:T(8,128)}) fusion(f32[1,64,16,5,512]{4,3,2,1,0:T(8,128)S(1)} %copy-done), kind=kLoop, calls=%fused_computation.54 | loop fusion | bytes 163840 | tf_op jit(solution)/shard_map/slice | solution.py:111
  211.4 3.0 copy.57
  214.4 3.0 copy.58
  217.4 3.0 collective-permute-start.2
  220.7 2.4 collective-permute-start.1
  223.1 3.5 collective-permute-start
  226.6 10.1 %collective-permute-start.3 = (f32[1,64,16,6,2]{1,2,4,3,0:T(8,128)S(1)}, f32[1,64,16,6,2]{1,2,4,3,0:T(8,128)S(1)}, u32[]{:S(2)}, u32[]{:S(2)}) collective-permute-start(f32[1,64,16,6,2]{1,2,4,3,0:T(8,128)S(1)} %get-tuple-element.196), channel_id=1, source_target_pairs={{4,0},{8,4},{12,8},{16,12},{20,16},{24,20},{28,24},{5,1},{9,5},{13... | collective-permute-start | bytes 147464 | tf_op jit(solution)/shard_map/ppermute | solution.py:15
  236.7 3.4 copy.77
  240.1 2.9 copy.74
  243.0 2.9 copy.76
  246.0 2.9 copy.75
  249.0 4.6 copy.63
  253.6 4.6 copy.68
  258.2 4.4 copy.64
  264.5 54.9 %fusion.6 = (f32[1,64,16,5,512]{4,3,2,1,0:T(8,128)}, f32[1,64,16,5,512]{4,3,2,1,0:T(8,128)}) fusion(f32[1,64,16,5,510]{4,3,2,1,0:T(8,128)} %multiply_add_fusion.1, f32[1,64,16,5,1]{4,3,2,1,0:T(8,128)} %copy.64, f32[1,64,16,5,1]{4,3,2,1,0:T(8,128)} %copy.63, f32[1,64,16,5,1]{4,3,2,1,0:T(8,128)} %copy.68, f32[1,64,16,5,512]{4,3,2,1,0:T(8,128)} %reshape.218, ...), kind=kLoop, calls=%fused_computation.20 | loop fusion | flops 102236160 | bytes 46649404 | tf_op jit(solution)/shard_map/div | solution.py:119
  319.4 8.0 %broadcast.170.clone = f32[1,64,16,5,512]{4,3,2,1,0:T(8,128)} broadcast(f32[]{:T(128)} %constant.48.clone.1), dimensions={} | broadcast | bytes 10485764 | tf_op jit(solution)/shard_map/broadcast.17
  327.4 7.9 %broadcast.170 = f32[1,64,16,5,512]{4,3,2,1,0:T(8,128)} broadcast(f32[]{:T(128)} %constant.48.clone.1), dimensions={} | broadcast | bytes 10485764 | tf_op jit(solution)/shard_map/broadcast.17
  335.2 134.5 %while.20 = (s32[]{:T(128)}, f32[1,64,16,5,512]{4,3,2,1,0:T(8,128)}, f32[1,64,16,5,512]{4,3,2,1,0:T(8,128)}, f32[1,16,5,512]{3,2,1,0:T(8,128)S(1)}, f32[1,16,5,5...) while((s32[]{:T(128)}, ...), condition=%wide.region_1.2_spmd.clone, body=%wide.region_0.1_spmd.clone.sunk | while | flops 204803 | bytes 1704051 | solution.py:138
  352.0 2.1 bitcast_dynamic-update-slice_fusion.3
  383.5 2.1 bitcast_dynamic-update-slice_fusion.3
  385.6 2.1 bitcast_dynamic-update-slice_fusion.3
  410.8 2.1 bitcast_dynamic-update-slice_fusion.3
  412.9 2.1 bitcast_dynamic-update-slice_fusion.3
  454.9 2.1 bitcast_dynamic-update-slice_fusion.3
  461.3 2.1 bitcast_dynamic-update-slice_fusion.3
  463.4 2.1 bitcast_dynamic-update-slice_fusion.3
  467.6 2.1 bitcast_dynamic-update-slice_fusion.3
  471.7 8.5 %collective-permute-done.4 = f32[1,16,5,512]{3,2,1,0:T(8,128)S(1)} collective-permute-done((f32[1,16,5,512]{3,2,1,0:T(8,128)S(1)}, f32[1,16,5,512]{3,2,1,0:T(8,128)S(1)}, u32[]{:S(2)}, u32[]{:S(2)}) %collective-permute-start.4) | collective-permute-done | bytes 163872 | tf_op jit(solution)/shard_map/ppermute | solution.py:23
  482.2 8.6 %collective-permute-done.5 = f32[1,16,5,512]{3,2,1,0:T(8,128)S(1)} collective-permute-done((f32[1,16,5,512]{3,2,1,0:T(8,128)S(1)}, f32[1,16,5,512]{3,2,1,0:T(8,128)S(1)}, u32[]{:S(2)}, u32[]{:S(2)}) %collective-permute-start.5) | collective-permute-done | bytes 163872 | tf_op jit(solution)/shard_map/ppermute | solution.py:23
  490.9 2.2 collective-permute-start.6
  493.1 6.1 %collective-permute-done.6 = f32[1,16,5,512]{3,2,1,0:T(8,128)S(1)} collective-permute-done((f32[1,16,5,512]{3,2,1,0:T(8,128)S(1)}, f32[1,16,5,512]{3,2,1,0:T(8,128)S(1)}, u32[]{:S(2)}, u32[]{:S(2)}) %collective-permute-start.6) | collective-permute-done | bytes 163872 | tf_op jit(solution)/shard_map/ppermute | solution.py:23
  499.2 23.8 %multiply_add_fusion = f32[1,64,16,5,512]{4,3,2,1,0:T(8,128)} fusion(f32[1,64,16,5,512]{4,3,2,1,0:T(8,128)} %get-tuple-element.133, f32[1,64,16,5,512]{4,3,2,1,0:T(8,128)} %reshape.218, f32[1,64,16,5,512]{4,3,2,1,0:T(8,128)} %get-tuple-element.132, f32[16,5,512]{2,1,0:T(8,128)S(1)} %bitcast.53), kind=kLoop, calls=%fused_computation.22 | loop fusion | flops 7864320 | bytes 42106880 | tf_op jit(solution)/shard_map/add | solution.py:143
  523.0 20.0 %copy.69 = f32[1,64,16,5,512]{4,2,3,1,0:T(8,128)} copy(f32[1,64,16,5,512]{4,3,2,1,0:T(8,128)} %multiply_add_fusion) | data formatting | bytes 20971520 | tf_op jit(solution)/shard_map/add | solution.py:143
  (115 shorter events, 127.3 us)
Async XLA Ops:
  52.4 26.5 %copy-start.1 = (s32[1,1,1,32,16]{3,4,2,1,0:T(8,128)S(1)}, s32[1,1,1,32,16]{3,4,2,1,0:T(8,128)}, u32[]{:S(2)}) copy-start(s32[1,1,1,32,16]{3,4,2,1,0:T(8,128)} %param.15) | copy-start | bytes 6148
  52.4 26.7 %copy-start.2 = (f32[1,1,1,32,16]{3,4,2,1,0:T(8,128)S(1)}, f32[1,1,1,32,16]{3,4,2,1,0:T(8,128)}, u32[]{:S(2)}) copy-start(f32[1,1,1,32,16]{3,4,2,1,0:T(8,128)} %param.17) | copy-start | bytes 6148
  52.4 26.8 %copy-start.3 = (s32[1,1,1,32,16]{3,4,2,1,0:T(8,128)S(1)}, s32[1,1,1,32,16]{3,4,2,1,0:T(8,128)}, u32[]{:S(2)}) copy-start(s32[1,1,1,32,16]{3,4,2,1,0:T(8,128)} %param.16) | copy-start | bytes 6148
  71.3 68.5 %all-to-all-start = ((f32[32,16,5,512]{3,1,2,0:T(8,128)}), f32[32,16,5,512]{3,1,2,0:T(8,128)}, u32[]{:S(2)}, u32[]{:S(2)}) async-start(f32[32,16,5,512]{3,1,2,0:T(8,128)} %copy.51), calls=%async_computation | async-start | bytes 10485760 | tf_op jit(solution)/shard_map/all_to_all | solution.py:46
  85.6 10.9 %copy-start.4 = (f32[5]{0:T(128)S(1)}, f32[5]{0:T(128)}, u32[]{:S(2)}) copy-start(f32[5]{0:T(128)} %param.12) | copy-start | bytes 64
  85.6 10.9 %copy-start.5 = (f32[5]{0:T(128)S(1)}, f32[5]{0:T(128)}, u32[]{:S(2)}) copy-start(f32[5]{0:T(128)} %param.13) | copy-start | bytes 64
  96.4 55.4 %slice-start = ((s8[5242880]{0:T(1024)(128)(4,1)}), s8[1048576]{0:T(1024)(128)(4,1)S(1)}, s32[]{:S(2)}) async-start(s8[5242880]{0:T(1024)(128)(4,1)} %bitcast.48), calls=%async_computation.1 | async-start | bytes 2097152
  146.7 5.2 slice-start.1
  182.4 10.4 %copy-start = (f32[1,64,16,5,512]{4,3,2,1,0:T(8,128)S(1)}, f32[1,64,16,5,512]{4,3,2,1,0:T(8,128)}, u32[]{:S(2)}) copy-start(f32[1,64,16,5,512]{4,3,2,1,0:T(8,128)} %reshape.218) | copy-start | bytes 31457284
  217.4 31.6 %collective-permute-start.2 = (f32[1,64,16,6,2]{1,2,4,3,0:T(8,128)S(1)}, f32[1,64,16,6,2]{1,2,4,3,0:T(8,128)S(1)}, u32[]{:S(2)}, u32[]{:S(2)}) collective-permute-start(f32[1,64,16,6,2]{1,2,4,3,0:T(8,128)S(1)} %get-tuple-element.197), channel_id=1, source_target_pairs={{0,4},{4,8},{8,12},{12,16},{16,20},{20,24},{24,28},{1,5},{5,9},{9,... | collective-permute-start | bytes 147464 | tf_op jit(solution)/shard_map/ppermute | solution.py:12
  220.7 43.8 %collective-permute-start.1 = (f32[1,2,16,6,512]{4,3,2,1,0:T(8,128)S(1)}, f32[1,2,16,6,512]{4,3,2,1,0:T(8,128)S(1)}, u32[]{:S(2)}, u32[]{:S(2)}) collective-permute-start(f32[1,2,16,6,512]{4,3,2,1,0:T(8,128)S(1)} %get-tuple-element.194), channel_id=1, source_target_pairs={{1,0},{2,1},{3,2},{5,4},{6,5},{7,6},{9,8},{10,9},{11,10},{13,12},{... | collective-permute-start | bytes 1179656 | tf_op jit(solution)/shard_map/ppermute | solution.py:15
  223.1 39.6 %collective-permute-start = (f32[1,2,16,6,512]{4,3,2,1,0:T(8,128)S(1)}, f32[1,2,16,6,512]{4,3,2,1,0:T(8,128)S(1)}, u32[]{:S(2)}, u32[]{:S(2)}) collective-permute-start(f32[1,2,16,6,512]{4,3,2,1,0:T(8,128)S(1)} %get-tuple-element.195), channel_id=1, source_target_pairs={{0,1},{1,2},{2,3},{4,5},{5,6},{6,7},{8,9},{9,10},{10,11},{12,13},{... | collective-permute-start | bytes 1179656 | tf_op jit(solution)/shard_map/ppermute | solution.py:12
  226.6 27.0 %collective-permute-start.3 = (f32[1,64,16,6,2]{1,2,4,3,0:T(8,128)S(1)}, f32[1,64,16,6,2]{1,2,4,3,0:T(8,128)S(1)}, u32[]{:S(2)}, u32[]{:S(2)}) collective-permute-start(f32[1,64,16,6,2]{1,2,4,3,0:T(8,128)S(1)} %get-tuple-element.196), channel_id=1, source_target_pairs={{4,0},{8,4},{12,8},{16,12},{20,16},{24,20},{28,24},{5,1},{9,5},{13... | collective-permute-start | bytes 147464 | tf_op jit(solution)/shard_map/ppermute | solution.py:15
  469.8 10.5 %collective-permute-start.4 = (f32[1,16,5,512]{3,2,1,0:T(8,128)S(1)}, f32[1,16,5,512]{3,2,1,0:T(8,128)S(1)}, u32[]{:S(2)}, u32[]{:S(2)}) collective-permute-start(f32[1,16,5,512]{3,2,1,0:T(8,128)S(1)} %multiply_add_fusion.5), channel_id=1, source_target_pairs={{0,1},{1,2},{2,3},{4,5},{5,6},{6,7},{8,9},{9,10},{10,11},{12,13},{... | collective-permute-start | bytes 491528 | tf_op jit(solution)/shard_map/ppermute | solution.py:23
  480.3 10.5 %collective-permute-start.5 = (f32[1,16,5,512]{3,2,1,0:T(8,128)S(1)}, f32[1,16,5,512]{3,2,1,0:T(8,128)S(1)}, u32[]{:S(2)}, u32[]{:S(2)}) collective-permute-start(f32[1,16,5,512]{3,2,1,0:T(8,128)S(1)} %multiply_add_fusion.4), channel_id=1, source_target_pairs={{0,1},{1,2},{2,3},{4,5},{5,6},{6,7},{8,9},{9,10},{10,11},{12,13},{... | collective-permute-start | bytes 491528 | tf_op jit(solution)/shard_map/ppermute | solution.py:23
  490.9 8.3 %collective-permute-start.6 = (f32[1,16,5,512]{3,2,1,0:T(8,128)S(1)}, f32[1,16,5,512]{3,2,1,0:T(8,128)S(1)}, u32[]{:S(2)}, u32[]{:S(2)}) collective-permute-start(f32[1,16,5,512]{3,2,1,0:T(8,128)S(1)} %multiply_add_fusion.3), channel_id=1, source_target_pairs={{0,1},{1,2},{2,3},{4,5},{5,6},{6,7},{8,9},{9,10},{10,11},{12,13},{... | collective-permute-start | bytes 491528 | tf_op jit(solution)/shard_map/ppermute | solution.py:23
where the time goes:
time: 554 us; the launch traced here: 543 us
  other arithmetic  226 us (41%)
  local copies, waits for them, and re-layouts  202 us (36%)
  waiting for transfers between devices  66.5 us (12%)
  starting transfers between devices  32.7 us (6%)
  matrix products  14.8 us (3%)
    dynamic_update_slice x64, other arithmetic, advance(): local_all = lax.dynamic_update_index_in_dim(local_all, run_local, index, 1)  134 us
    unnamed x29, local copies, waits for them, and re-layouts  59.9 us
    div x1, other arithmetic, on_device(): source = 100.0 * residual / (1.0 + courant)  54.9 us
    all_to_all x1, waiting for transfers between devices, on_device(): lax.all_to_all(direct, ('block', 'span'), split_axis=0, concat_axis=0, ti...  43.3 us
    add x1, other arithmetic, on_device(): return filled + local_part + growth * inflow[:, None]  23.8 us
    ppermute x3, waiting for transfers between devices, from_behind(): return lax.ppermute(block, axis, route)  23.2 us
    add x1, local copies, waits for them, and re-layouts, on_device(): return filled + local_part + growth * inflow[:, None]  20 us
    reshape x2, local copies, waits for them, and re-layouts, on_device(): direct = outgoing.reshape(peer_count, capacity, components, width_z)  18.9 us
  transfers between devices with their start and end apart: 8, of which 4 were waited for; matrix products, arithmetic and copies ran while one was open for 8% of the time, Pallas kernels for 0%

commit v1 on v0

v1 whole, which is shorter than its diff:
```python
import functools

import jax
import jax.numpy as jnp
from jax import lax
from jax.experimental import pallas as pl
from jax.experimental.pallas import tpu as pltpu
from jax.sharding import PartitionSpec as P

MESH = pl.DeviceIdType.MESH
STRIDE = 11
UNROLL = 4


def limited(first_diff, second_diff):
    low = jnp.minimum(second_diff, 0.0)
    high = jnp.maximum(second_diff, 0.0)
    return jnp.minimum(jnp.maximum(first_diff, low), high)


def kernel(
    sizes,
    flow,
    speed,
    scale,
    ratio,
    send_tile,
    recv_tile,
    recv_live,
    weight,
    out,
    field,
    filled,
    donors,
    tiles,
    ws,
    inverse,
    growth,
    blend,
    sending,
    arriving,
    packed,
    row_low,
    row_high,
    col_low,
    col_high,
    last_update,
    last_growth,
    update_in,
    growth_in,
    slot_vmem,
    slot_of,
    load_sem,
    send_sem,
    recv_sem,
    halo_send,
    halo_recv,
    relay_send,
    relay_recv,
    out_sem,
    misc_sem,
):
    blocks, spans, streams = sizes
    width, parts, rows, lanes = flow.shape[0], flow.shape[1], flow.shape[2], 128
    peers = blocks * spans
    capacity = send_tile.shape[0]
    tiles_z = rows // 16
    chips = spans // 2
    message = capacity * tiles_z
    b = lax.axis_index("block")
    s = lax.axis_index("span")
    t = lax.axis_index("stream")
    me = b * spans + s
    z, core = s // 2, s % 2
    sign = 1 - 2 * core

    def partner(k):
        offset = (k * STRIDE) % peers
        to_block = (b + sign * (offset // spans) + blocks) % blocks
        to_chip = (z + sign * ((offset % spans) // 2) + chips) % chips
        to_core = (core + offset % 2) % 2
        return to_block, to_chip * 2 + to_core

    def at_stream(target):
        return (b, s, target)

    def load(v):
        return pltpu.make_async_copy(flow.at[:, v], field.at[v], load_sem.at[v])

    first_load = pltpu.make_async_copy(flow.at[:, 0], filled.at[pl.ds(0, width)], misc_sem.at[0])
    first_load.start()
    speed_load = pltpu.make_async_copy(speed, ws.at[pl.ds(1, width)], misc_sem.at[1])
    speed_load.start()
    for v in range(parts):
        load(v).start()

    barrier = pltpu.get_barrier_semaphore()

    def greet(k, carry):
        to_block, to_span = partner(k)
        pl.semaphore_signal(
            barrier, inc=1, device_id=(to_block, to_span, t), device_id_type=MESH
        )
        return carry

    lax.fori_loop(1, peers, greet, 0)
    for j in range(1, streams):
        pl.semaphore_signal(
            barrier, inc=1, device_id=at_stream((t + j) % streams), device_id_type=MESH
        )

    def donor_copy(v, k):
        to_block, to_span = partner(k)
        return pltpu.make_async_remote_copy(
            src_ref=sending.at[v, k],
            dst_ref=arriving.at[v, me],
            send_sem=send_sem.at[v],
            recv_sem=recv_sem.at[v],
            device_id=(to_block, to_span, t),
            device_id_type=MESH,
        )

    def send_all(v, source):
        def lay(x, carry):
            for y in range(16):
                row = pl.ds((y // 8) * 8 * tiles_z + y % 8, tiles_z, stride=8)
                tiles[x * 16 + y] = filled[x, row, :] if source is filled else source[v, x, row, :]
            return carry

        lax.fori_loop(0, width, lay, 0)
        for c in range(capacity):
            arriving[v, me, pl.ds(c * tiles_z, tiles_z), :] = tiles[send_tile[c, me]]

        def one(k, carry):
            to_block, to_span = partner(k)
            peer = to_block * spans + to_span
            for c in range(capacity):
                sending[v, k, pl.ds(c * tiles_z, tiles_z), :] = tiles[send_tile[c, peer]]
            donor_copy(v, k).start()
            return carry

        lax.fori_loop(1, peers, one, 0)

    first_load.wait()
    pl.semaphore_wait(barrier, peers - 1 + streams - 1)
    send_all(0, filled)

    speed_load.wait()
    speed_halo = pltpu.make_async_remote_copy(
        src_ref=ws.at[width],
        dst_ref=ws.at[0],
        send_sem=misc_sem.at[2],
        recv_sem=misc_sem.at[3],
        device_id=at_stream((t + 1) % streams),
        device_id_type=MESH,
    )

    @pl.when(t < streams - 1)
    def _():
        speed_halo.start()

    for v in range(parts):
        load(v).wait()
    send_all(1, field)

    @pl.when(t == 0)
    def _():
        ws[0] = jnp.zeros((rows, lanes), jnp.float32)
        row_low[...] = jnp.zeros(row_low.shape, jnp.float32)

    @pl.when(t == streams - 1)
    def _():
        row_high[...] = jnp.zeros(row_high.shape, jnp.float32)

    @pl.when(s == 0)
    def _():
        col_low[...] = jnp.zeros(col_low.shape, jnp.float32)

    @pl.when(s == spans - 1)
    def _():
        col_high[...] = jnp.zeros(col_high.shape, jnp.float32)

    lane = lax.broadcasted_iota(jnp.int32, (8, lanes), 1)
    tile_id = lane * 8 + lax.broadcasted_iota(jnp.int32, (8, lanes), 0)

    def place(g, carry):
        slots, weights = carry
        for c in range(capacity):
            target = jnp.where(recv_live[c, g] == 1, recv_tile[c, g], -1)
            hit = tile_id == target
            slots = jnp.where(hit, g * capacity + c, slots)
            weights = jnp.where(hit, weight[c, g], weights)
        return slots, weights

    slots, weights = lax.fori_loop(
        0,
        peers,
        place,
        (jnp.zeros((8, lanes), jnp.int32), jnp.zeros((8, lanes), jnp.float32)),
    )
    slot_vmem[...] = slots
    to_scalar = pltpu.make_async_copy(slot_vmem, slot_of, misc_sem.at[4])
    to_scalar.start()

    def spread(x, weights):
        for half in range(2):
            blend[x, pl.ds(half * 8, 8), :] = jnp.broadcast_to(weights[:, 0:1], (8, lanes))
            weights = pltpu.roll(weights, lanes - 1, 1)
        return weights

    lax.fori_loop(0, width, spread, weights)
    to_scalar.wait()

    @pl.when(t > 0)
    def _():
        speed_halo.wait_recv()

    tile_rows = [pl.ds(i * 8, 8) for i in range(rows // 8)]

    def factors(v):
        rate = scale[v]
        slot = v % 2

        def one(x, carry):
            new = []
            for i, r in enumerate(tile_rows):
                prior = rate * ws[x, r, :]
                here = rate * ws[x + 1, r, :]
                inv = 100.0 / (1.0 + 100.0 * here)
                inverse[x, r, :] = inv
                grown = carry[i] * (prior * inv)
                growth[slot, x, r, :] = grown
                new.append(grown)
            return tuple(new)

        ones = tuple(jnp.ones((8, lanes), jnp.float32) for _ in tile_rows)
        ended = lax.fori_loop(0, width, one, ones)
        for r, grown in zip(tile_rows, ended):
            last_growth[v, r, :] = grown

    def relay(v, kind, j):
        source = last_growth if kind else last_update
        target = growth_in if kind else update_in
        return pltpu.make_async_remote_copy(
            src_ref=source.at[v],
            dst_ref=target.at[v, t],
            send_sem=relay_send.at[v, kind, j],
            recv_sem=relay_recv.at[v, kind, t],
            device_id=at_stream((t + j) % streams),
            device_id_type=MESH,
        )

    def relay_from(v, kind, source):
        target = growth_in if kind else update_in
        return pltpu.make_async_copy(
            target.at[v, source], target.at[v, source], relay_recv.at[v, kind, source]
        )

    def relay_all(v, kind):
        for j in range(1, streams):

            @pl.when(t + j < streams)
            def _():
                relay(v, kind, j).start()

    def fill(v):
        def take_peer(g, carry):
            for c in range(capacity):
                donors[g * capacity + c] = arriving[v, g, pl.ds(c * tiles_z, tiles_z), :]
            return carry

        lax.fori_loop(0, peers, take_peer, 0)

        def scatter(x, carry):
            for y in range(16):
                row = pl.ds((y // 8) * 8 * tiles_z + y % 8, tiles_z, stride=8)
                filled[x, row, :] = donors[slot_of[y % 8, x * 2 + y // 8]]
            return carry

        lax.fori_loop(0, width, scatter, 0)

        def mix(x, carry):
            first, before, last = carry
            for half in range(2):
                w = blend[x, pl.ds(half * 8, 8), :]
                rest = 1.0 - w
                kept = []
                for i in range(tiles_z):
                    r = tile_rows[half * tiles_z + i]
                    value = rest * field[v, x, r, :] + w * filled[x, r, :]
                    filled[x, r, :] = value
                    kept.append(value)
                i = x * 2 + half
                here = lane == i
                first = jnp.where(here, pltpu.roll(kept[0], i, 1), first)
                before = jnp.where(here, pltpu.roll(kept[-1], (i + 2) % lanes, 1), before)
                last = jnp.where(here, pltpu.roll(kept[-1], (i + 1) % lanes, 1), last)
            return first, before, last

        zero = jnp.zeros((8, lanes), jnp.float32)
        for i, value in enumerate(lax.fori_loop(0, width, mix, (zero, zero, zero))):
            packed[v, i] = value

    def halo_copy(v, kind):
        src, dst, target = (
            (filled.at[pl.ds(width - 2, 2)], row_low.at[v], (b, s, (t + 1) % streams)),
            (filled.at[0], row_high.at[v], (b, s, (t + streams - 1) % streams)),
            (packed.at[v, pl.ds(1, 2)], col_low.at[v], (b, (s + 1) % spans, t)),
            (packed.at[v, 0], col_high.at[v], (b, (s + spans - 1) % spans, t)),
        )[kind]
        return pltpu.make_async_remote_copy(
            src_ref=src,
            dst_ref=dst,
            send_sem=halo_send.at[v, kind],
            recv_sem=halo_recv.at[v, kind],
            device_id=target,
            device_id_type=MESH,
        )

    sends = (t < streams - 1, t > 0, s < spans - 1, s > 0)
    receives = (t > 0, t < streams - 1, s > 0, s < spans - 1)

    def halos(v, which, act):
        for kind in range(4):

            @pl.when(which[kind])
            def _():
                act(halo_copy(v, kind))

    def sweep(v):
        rate = scale[v]
        rate_z = rate * ratio[v]
        is_first = lane == 0
        is_last = lane == lanes - 1
        before2, before1, after1 = col_low[v, 0], col_low[v, 1], col_high[v]
        edge_first = packed[v, 0] - before1
        edge_face = before1 + 0.5 * limited(before1 - before2, edge_first)
        edge_last = after1 - packed[v, 2]
        for i, r in enumerate(tile_rows):
            filled[width, r, :] = row_high[v, r, :]

        for half in range(2):
            mine = tile_rows[half * tiles_z : (half + 1) * tiles_z]

            def step(x, carry, end):
                cells, diffs, flux, e_first, e_face, e_last = carry
                n = range(tiles_z)
                right = [pltpu.roll(u, 1, 1) for u in cells]
                e = [
                    cells[i] - jnp.where(is_first, right[i - 1], right[i]) if i else None for i in n
                ]
                e[0] = jnp.where(is_first, e_first, cells[0] - right[0])
                left = [pltpu.roll(d, lanes - 1, 1) for d in e]
                ahead = [
                    jnp.where(is_last, left[i + 1] if i + 1 < tiles_z else e_last, left[i])
                    for i in n
                ]
                face = [cells[i] + 0.5 * limited(e[i], ahead[i]) for i in n]
                shifted = [pltpu.roll(f, 1, 1) for f in face]
                behind = [
                    jnp.where(is_first, shifted[i - 1] if i else e_face, shifted[i]) for i in n
                ]
                span_term = [rate_z * (behind[i] - face[i]) for i in n]
                coming = [filled[x + 1, r, :] for r in mine]
                next_diffs = [coming[i] - cells[i] for i in n]
                face_x = [cells[i] + 0.5 * limited(diffs[i], next_diffs[i]) for i in n]
                speed_x = [rate * ws[x + 1, r, :] for r in mine]
                rest = [span_term[i] - speed_x[i] * face_x[i] for i in n]
                update = [inverse[x, r, :] * (flux[i] + rest[i]) for i, r in enumerate(mine)]
                next_flux = [speed_x[i] * (update[i] + face_x[i]) for i in n]
                for i, r in enumerate(mine):
                    field[v, x, r, :] = cells[i] + update[i]
                    if end:
                        last_update[v, r, :] = update[i]
                return (
                    coming,
                    next_diffs,
                    next_flux,
                    pltpu.roll(e_first, lanes - 2, 1),
                    pltpu.roll(e_face, lanes - 2, 1),
                    pltpu.roll(e_last, lanes - 2, 1),
                )

            def steps(outer, carry):
                for k in range(UNROLL):
                    carry = step(outer * UNROLL + k, carry, k == UNROLL - 1)
                return carry

            cells = [filled[0, r, :] for r in mine]
            up1 = [row_low[v, 1, r, :] for r in mine]
            up2 = [row_low[v, 0, r, :] for r in mine]
            diffs = [c - u for c, u in zip(cells, up1)]
            flux = [
                rate * ws[0, r, :] * (u + 0.5 * limited(u - u2, d))
                for r, u, u2, d in zip(mine, up1, up2, diffs)
            ]

            def turned(value, shift):
                return pltpu.roll(value, shift, 1) if shift else value

            lax.fori_loop(
                0,
                width // UNROLL,
                steps,
                (
                    cells,
                    diffs,
                    flux,
                    turned(edge_first, (lanes - half) % lanes),
                    turned(edge_face, (lanes - half) % lanes),
                    turned(edge_last, lanes - 1 - half),
                ),
            )

    def finish(v):
        slot = v % 2
        for j in range(streams - 1):

            @pl.when(j < t)
            def _():
                relay_from(v, 0, j).wait()
                relay_from(v, 1, j).wait()

        inflow = [jnp.zeros((8, lanes), jnp.float32) for _ in tile_rows]
        for j in range(streams - 1):
            inflow = [
                jnp.where(
                    j < t, growth_in[v, j, r, :] * inflow[i] + update_in[v, j, r, :], inflow[i]
                )
                for i, r in enumerate(tile_rows)
            ]

        def one(x, carry):
            for i, r in enumerate(tile_rows):
                field[v, x, r, :] = field[v, x, r, :] + growth[slot, x, r, :] * inflow[i]
            return carry

        lax.fori_loop(0, width, one, 0)
        out_copy(v).start()

    def out_copy(v):
        return pltpu.make_async_copy(field.at[v], out.at[:, v], out_sem.at[v])

    def all_donors(v):
        return pltpu.make_async_remote_copy(
            src_ref=sending.at[v, pl.ds(1, peers - 1)],
            dst_ref=arriving.at[v, pl.ds(0, peers - 1)],
            send_sem=send_sem.at[v],
            recv_sem=recv_sem.at[v],
            device_id=(b, s, (t + 1) % streams),
            device_id_type=MESH,
        )

    def variable(v, carry):
        factors(v)
        relay_all(v, 1)
        all_donors(v).wait_recv()
        fill(v)
        halos(v, sends, lambda copy: copy.start())

        @pl.when(v + 2 < parts)
        def _():
            send_all(v + 2, field)

        @pl.when(v > 0)
        def _():
            finish(v - 1)

        halos(v, receives, lambda copy: copy.wait_recv())
        sweep(v)
        relay_all(v, 0)
        halos(v, sends, lambda copy: copy.wait_send())
        return carry

    lax.fori_loop(0, parts, variable, 0)
    finish(parts - 1)

    for v in range(parts):
        all_donors(v).wait_send()
        for kind in range(2):
            for j in range(1, streams):

                @pl.when(t + j < streams)
                def _():
                    relay(v, kind, j).wait_send()

        out_copy(v).wait()

    @pl.when(t < streams - 1)
    def _():
        speed_halo.wait_send()


def on_device(
    flow_state, wave_speed, char_scale, span_ratio, send_tile, recv_tile, recv_live, interp_weight
):
    sizes = tuple(lax.axis_size(a) for a in ("block", "span", "stream"))
    blocks, spans, streams = sizes
    _, width, rows_y, parts, width_z = flow_state.shape
    tiles_z = width_z // 128
    rows = rows_y * tiles_z
    capacity = send_tile.shape[-1]
    peers = blocks * spans

    def tiled(array):
        lead = array.shape[:-2]
        array = array.reshape(lead + (rows_y // 8, 8, tiles_z, 128))
        return jnp.swapaxes(array, -3, -2).reshape(lead + (rows, 128))

    flow = tiled(jnp.transpose(flow_state[0], (0, 2, 1, 3)))
    speed = tiled(wave_speed[0])
    small = [
        jnp.transpose(a.reshape(peers, capacity))
        for a in (send_tile, recv_tile, recv_live, interp_weight)
    ]
    f32 = jnp.float32
    anywhere = pl.BlockSpec(memory_space=pl.ANY)
    scalars = pl.BlockSpec(memory_space=pltpu.SMEM)
    message = capacity * tiles_z
    vmem = lambda *shape: pltpu.VMEM(shape, f32)
    dma = pltpu.SemaphoreType.DMA
    result = pl.pallas_call(
        functools.partial(kernel, sizes),
        out_shape=jax.ShapeDtypeStruct(flow.shape, f32),
        in_specs=[anywhere, anywhere] + [scalars] * 6,
        out_specs=anywhere,
        scratch_shapes=[
            vmem(parts, width, rows, 128),
            vmem(width + 1, rows, 128),
            vmem(peers * capacity, tiles_z, 128),
            vmem(width * rows_y, tiles_z, 128),
            vmem(width + 1, rows, 128),
            vmem(width, rows, 128),
            vmem(2, width, rows, 128),
            vmem(width, rows_y, 128),
            vmem(parts, peers, message, 128),
            vmem(parts, peers, message, 128),
            vmem(parts, 3, 8, 128),
            vmem(parts, 2, rows, 128),
            vmem(parts, rows, 128),
            vmem(parts, 2, 8, 128),
            vmem(parts, 8, 128),
            vmem(parts, rows, 128),
            vmem(parts, rows, 128),
            vmem(parts, streams, rows, 128),
            vmem(parts, streams, rows, 128),
            pltpu.VMEM((8, 128), jnp.int32),
            pltpu.SMEM((8, 128), jnp.int32),
            dma((parts,)),
            dma((parts,)),
            dma((parts,)),
            dma((parts, 4)),
            dma((parts, 4)),
            dma((parts, 2, streams)),
            dma((parts, 2, streams)),
            dma((parts,)),
            dma((5,)),
        ],
        compiler_params=pltpu.CompilerParams(
            collective_id=1, has_side_effects=True, vmem_limit_bytes=56 * 1024 * 1024
        ),
        name="overset_step",
    )(flow, speed, char_scale, span_ratio, *small)
    result = result.reshape(width, parts, rows_y // 8, tiles_z, 8, 128)
    result = jnp.swapaxes(result, 3, 4).reshape(width, parts, rows_y, width_z)
    return jnp.transpose(result, (0, 2, 1, 3))[None]


def solution(mesh):
    return jax.shard_map(
        on_device,
        mesh=mesh,
        in_specs=(
            P("block", "stream", None, None, "span"),
            P("block", "stream", None, "span"),
            P(),
            P(),
            P("block", "span", "stream", None, None),
            P("block", "span", "stream", None, None),
            P("block", "span", "stream", None, None),
            P("block", "span", "stream", None, None),
        ),
        out_specs=P("block", "stream", None, None, "span"),
        check_vma=False,
    )
```

time: 554 us -> 156 us (0.28)
  the two profiles are of different devices: /device:TPU:80 before, /device:TPU:58 now
where the time goes in v1:
time: 156 us; the launch traced here: 154 us
  Pallas kernels  143 us (92%)
  local copies, waits for them, and re-layouts  10.5 us (7%)
    pallas_call x1, Pallas kernels, on_device(): pl.pallas_call(functools.partial(kernel, sizes), out_shape=jax.ShapeDtype...  143 us
    unnamed x1, local copies, waits for them, and re-layouts  10.5 us

profile of v1, /device:TPU:58, one launch (start us, length us, event | category | flops | bytes accessed | tf_op | source)
XLA Modules:
  0.0 153.9 jit_solution(15362520941649905999)
XLA Ops:
  0.0 143.3 %overset_step.1 = f32[64,5,64,128]{3,2,1,0:T(8,128)} custom-call(f32[64,5,64,128]{3,2,1,0:T(8,128)} %bitcast.36, f32[64,64,128]{2,1,0:T(8,128)} %bitcast.37, f32[5]{0:T(128)} %scale.1, f32[5]{0:T(128)} %ratio.1, s32[16,32]{1,0:T(8,128)} %bitcast.38, s32[16,32]{1,0:T(8,128)} %bitcast.39, s32[16,32]{1,0:T(8,128)} %bitcast.40, f32[16,32]{1,0:T(8,128)} %bitcast.41), custom_call_target="tpu_custom_call" | custom-call | tf_op jit(solution)/shard_map/overset_step/pallas_call | solution.py:522
  143.3 10.5 %copy.10 = f32[1,64,16,5,512]{4,2,3,1,0:T(8,128)} copy(f32[1,64,16,5,512]{4,2,3,1,0:T(8,128)} %bitcast.35) | data formatting | bytes 20971520

commit v2 on v1

--- a/solution.py
+++ b/solution.py
@@ -9,7 +9,8 @@
 
 MESH = pl.DeviceIdType.MESH
 STRIDE = 11
-UNROLL = 4
+UNROLL = 8
+TURN = 4
 
 
 def limited(first_diff, second_diff):
@@ -202,13 +203,16 @@
     to_scalar = pltpu.make_async_copy(slot_vmem, slot_of, misc_sem.at[4])
     to_scalar.start()
 
-    def spread(x, weights):
-        for half in range(2):
-            blend[x, pl.ds(half * 8, 8), :] = jnp.broadcast_to(weights[:, 0:1], (8, lanes))
-            weights = pltpu.roll(weights, lanes - 1, 1)
+    def spread(outer, weights):
+        for k in range(2 * TURN):
+            i = outer * 2 * TURN + k
+            turned = pltpu.roll(weights, (lanes - i) % lanes, 1)
+            blend[outer * TURN + k // 2, pl.ds(k % 2 * 8, 8), :] = jnp.broadcast_to(
+                turned[:, 0:1], (8, lanes)
+            )
         return weights
 
-    lax.fori_loop(0, width, spread, weights)
+    lax.fori_loop(0, width // TURN, spread, weights)
     to_scalar.wait()
 
     @pl.when(t > 0)
@@ -279,9 +283,10 @@
 
         lax.fori_loop(0, width, scatter, 0)
 
-        def mix(x, carry):
+        def mix(outer, carry):
             first, before, last = carry
-            for half in range(2):
+            for k in range(2 * TURN):
+                x, half = outer * TURN + k // 2, k % 2
                 w = blend[x, pl.ds(half * 8, 8), :]
                 rest = 1.0 - w
                 kept = []
@@ -290,7 +295,7 @@
                     value = rest * field[v, x, r, :] + w * filled[x, r, :]
                     filled[x, r, :] = value
                     kept.append(value)
-                i = x * 2 + half
+                i = outer * 2 * TURN + k
                 here = lane == i
                 first = jnp.where(here, pltpu.roll(kept[0], i, 1), first)
                 before = jnp.where(here, pltpu.roll(kept[-1], (i + 2) % lanes, 1), before)
@@ -298,7 +303,7 @@
             return first, before, last
 
         zero = jnp.zeros((8, lanes), jnp.float32)
-        for i, value in enumerate(lax.fori_loop(0, width, mix, (zero, zero, zero))):
+        for i, value in enumerate(lax.fori_loop(0, width // TURN, mix, (zero, zero, zero))):
             packed[v, i] = value
 
     def halo_copy(v, kind):
@@ -333,9 +338,7 @@
         is_first = lane == 0
         is_last = lane == lanes - 1
         before2, before1, after1 = col_low[v, 0], col_low[v, 1], col_high[v]
-        edge_first = packed[v, 0] - before1
-        edge_face = before1 + 0.5 * limited(before1 - before2, edge_first)
-        edge_last = after1 - packed[v, 2]
+        edge_face = before1 + 0.5 * limited(before1 - before2, packed[v, 0] - before1)
         for i, r in enumerate(tile_rows):
             filled[width, r, :] = row_high[v, r, :]
 
@@ -343,22 +346,23 @@
             mine = tile_rows[half * tiles_z : (half + 1) * tiles_z]
 
             def step(x, carry, end):
-                cells, diffs, flux, e_first, e_face, e_last = carry
+                cells, diffs, flux = carry
                 n = range(tiles_z)
+                i = x * 2 + half
+                to_first = (lanes - i) % lanes
+                outside = pltpu.roll(before1, to_first, 1)
+                outside_face = pltpu.roll(edge_face, to_first, 1)
+                beyond = pltpu.roll(after1, lanes - 1 - i, 1)
                 right = [pltpu.roll(u, 1, 1) for u in cells]
-                e = [
-                    cells[i] - jnp.where(is_first, right[i - 1], right[i]) if i else None for i in n
+                left = [pltpu.roll(u, lanes - 1, 1) for u in cells]
+                low = [jnp.where(is_first, ([outside] + right)[i], right[i]) for i in n]
+                high = [jnp.where(is_last, (left + [beyond])[i + 1], left[i]) for i in n]
+                face = [
+                    cells[i] + 0.5 * limited(cells[i] - low[i], high[i] - cells[i]) for i in n
                 ]
-                e[0] = jnp.where(is_first, e_first, cells[0] - right[0])
-                left = [pltpu.roll(d, lanes - 1, 1) for d in e]
-                ahead = [
-                    jnp.where(is_last, left[i + 1] if i + 1 < tiles_z else e_last, left[i])
-                    for i in n
-                ]
-                face = [cells[i] + 0.5 * limited(e[i], ahead[i]) for i in n]
                 shifted = [pltpu.roll(f, 1, 1) for f in face]
                 behind = [
-                    jnp.where(is_first, shifted[i - 1] if i else e_face, shifted[i]) for i in n
+                    jnp.where(is_first, ([outside_face] + shifted)[i], shifted[i]) for i in n
                 ]
                 span_term = [rate_z * (behind[i] - face[i]) for i in n]
                 coming = [filled[x + 1, r, :] for r in mine]
@@ -372,14 +376,7 @@
                     field[v, x, r, :] = cells[i] + update[i]
                     if end:
                         last_update[v, r, :] = update[i]
-                return (
-                    coming,
-                    next_diffs,
-                    next_flux,
-                    pltpu.roll(e_first, lanes - 2, 1),
-                    pltpu.roll(e_face, lanes - 2, 1),
-                    pltpu.roll(e_last, lanes - 2, 1),
-                )
+                return coming, next_diffs, next_flux
 
             def steps(outer, carry):
                 for k in range(UNROLL):
@@ -395,22 +392,7 @@
                 for r, u, u2, d in zip(mine, up1, up2, diffs)
             ]
 
-            def turned(value, shift):
-                return pltpu.roll(value, shift, 1) if shift else value
-
-            lax.fori_loop(
-                0,
-                width // UNROLL,
-                steps,
-                (
-                    cells,
-                    diffs,
-                    flux,
-                    turned(edge_first, (lanes - half) % lanes),
-                    turned(edge_face, (lanes - half) % lanes),
-                    turned(edge_last, lanes - 1 - half),
-                ),
-            )
+            lax.fori_loop(0, width // UNROLL, steps, (cells, diffs, flux))
 
     def finish(v):
         slot = v % 2

time: 156 us -> 106 us (0.68)
  Pallas kernels: 143 us -> 94.8 us
    pallas_call x1, Pallas kernels: 143 us -> 94.8 us  [on_device(): pl.pallas_call(functools.partial(kernel, sizes), out_shape=jax.ShapeDtype...]
where the time goes in v2:
time: 106 us; the launch traced here: 105 us
  Pallas kernels  94.8 us (89%)
  local copies, waits for them, and re-layouts  10.5 us (10%)
    pallas_call x1, Pallas kernels, on_device(): pl.pallas_call(functools.partial(kernel, sizes), out_shape=jax.ShapeDtype...  94.8 us
    unnamed x1, local copies, waits for them, and re-layouts  10.5 us

profile of v2, /device:TPU:58, one launch (start us, length us, event | category | flops | bytes accessed | tf_op | source)
XLA Modules:
  0.0 105.3 jit_solution(5660687438485025873)
XLA Ops:
  0.0 94.8 %overset_step.1 = f32[64,5,64,128]{3,2,1,0:T(8,128)} custom-call(f32[64,5,64,128]{3,2,1,0:T(8,128)} %bitcast.36, f32[64,64,128]{2,1,0:T(8,128)} %bitcast.37, f32[5]{0:T(128)} %scale.1, f32[5]{0:T(128)} %ratio.1, s32[16,32]{1,0:T(8,128)} %bitcast.38, s32[16,32]{1,0:T(8,128)} %bitcast.39, s32[16,32]{1,0:T(8,128)} %bitcast.40, f32[16,32]{1,0:T(8,128)} %bitcast.41), custom_call_target="tpu_custom_call" | custom-call | tf_op jit(solution)/shard_map/overset_step/pallas_call | solution.py:504
  94.8 10.5 %copy.10 = f32[1,64,16,5,512]{4,2,3,1,0:T(8,128)} copy(f32[1,64,16,5,512]{4,2,3,1,0:T(8,128)} %bitcast.35) | data formatting | bytes 20971520

commit v3 on v2

--- a/solution.py
+++ b/solution.py
@@ -29,7 +29,6 @@
     recv_tile,
     recv_live,
     weight,
-    out,
     field,
     filled,
     donors,
@@ -58,7 +57,6 @@
     halo_recv,
     relay_send,
     relay_recv,
-    out_sem,
     misc_sem,
 ):
     blocks, spans, streams = sizes
@@ -129,6 +127,8 @@
             return carry
 
         lax.fori_loop(0, width, lay, 0)
+        if source is filled:
+            pl.semaphore_wait(barrier, peers - 1 + streams - 1)
         for c in range(capacity):
             arriving[v, me, pl.ds(c * tiles_z, tiles_z), :] = tiles[send_tile[c, me]]
 
@@ -143,7 +143,6 @@
         lax.fori_loop(1, peers, one, 0)
 
     first_load.wait()
-    pl.semaphore_wait(barrier, peers - 1 + streams - 1)
     send_all(0, filled)
 
     speed_load.wait()
@@ -418,10 +417,6 @@
             return carry
 
         lax.fori_loop(0, width, one, 0)
-        out_copy(v).start()
-
-    def out_copy(v):
-        return pltpu.make_async_copy(field.at[v], out.at[:, v], out_sem.at[v])
 
     def all_donors(v):
         return pltpu.make_async_remote_copy(
@@ -466,11 +461,20 @@
                 def _():
                     relay(v, kind, j).wait_send()
 
-        out_copy(v).wait()
-
     @pl.when(t < streams - 1)
     def _():
         speed_halo.wait_send()
+
+
+def write_out(result, out, sems):
+    copies = [
+        pltpu.make_async_copy(result.at[v], out.at[:, v], sems.at[v])
+        for v in range(result.shape[0])
+    ]
+    for copy in copies:
+        copy.start()
+    for copy in copies:
+        copy.wait()
 
 
 def on_device(
@@ -503,11 +507,10 @@
     dma = pltpu.SemaphoreType.DMA
     result = pl.pallas_call(
         functools.partial(kernel, sizes),
-        out_shape=jax.ShapeDtypeStruct(flow.shape, f32),
+        out_shape=pltpu.VMEM((parts, width, rows, 128), f32),
         in_specs=[anywhere, anywhere] + [scalars] * 6,
-        out_specs=anywhere,
+        out_specs=pl.BlockSpec(memory_space=pltpu.VMEM),
         scratch_shapes=[
-            vmem(parts, width, rows, 128),
             vmem(width + 1, rows, 128),
             vmem(peers * capacity, tiles_z, 128),
             vmem(width * rows_y, tiles_z, 128),
@@ -535,14 +538,22 @@
             dma((parts, 4)),
             dma((parts, 2, streams)),
             dma((parts, 2, streams)),
-            dma((parts,)),
             dma((5,)),
         ],
         compiler_params=pltpu.CompilerParams(
-            collective_id=1, has_side_effects=True, vmem_limit_bytes=56 * 1024 * 1024
+            collective_id=1, has_side_effects=True, vmem_limit_bytes=44 * 1024 * 1024
         ),
         name="overset_step",
     )(flow, speed, char_scale, span_ratio, *small)
+    result = pl.pallas_call(
+        write_out,
+        out_shape=jax.ShapeDtypeStruct(flow.shape, f32),
+        in_specs=[pl.BlockSpec(memory_space=pltpu.VMEM)],
+        out_specs=pl.BlockSpec(memory_space=pltpu.HBM),
+        scratch_shapes=[dma((parts,))],
+        compiler_params=pltpu.CompilerParams(vmem_limit_bytes=8 * 1024 * 1024),
+        name="write_out",
+    )(pltpu.with_memory_space_constraint(result, pltpu.VMEM))
     result = result.reshape(width, parts, rows_y // 8, tiles_z, 8, 128)
     result = jnp.swapaxes(result, 3, 4).reshape(width, parts, rows_y, width_z)
     return jnp.transpose(result, (0, 2, 1, 3))[None]

time: 106 us -> 96.6 us (0.911)
  local copies, waits for them, and re-layouts: 10.5 us -> 0 us
  Pallas kernels: 94.8 us -> 96.4 us
    unnamed x1 -> x0, local copies, waits for them, and re-layouts: 10.5 us -> none
    pallas_call x1 -> x2, Pallas kernels: 94.8 us -> 96.4 us  [the longest x1 92.4 us: on_device(): pl.pallas_call(functools.partial(kernel, sizes), out_shape=pltpu.VMEM((pa...]
where the time goes in v3:
time: 96.6 us; the launch traced here: 96.4 us
  Pallas kernels  96.4 us (100%)
    pallas_call x1, Pallas kernels, on_device(): pl.pallas_call(functools.partial(kernel, sizes), out_shape=pltpu.VMEM((pa...  92.4 us
    pallas_call x1, Pallas kernels, on_device(): pl.pallas_call(write_out, out_shape=jax.ShapeDtypeStruct(flow.shape, f32)...  4.01 us

profile of v3, /device:TPU:58, one launch (start us, length us, event | category | flops | bytes accessed | tf_op | source)
XLA Modules:
  0.0 96.4 jit_solution(5599694683636696169)
XLA Ops:
  0.0 92.4 %overset_step.1.result = f32[5,64,64,128]{3,2,1,0:T(8,128)S(1)} custom-call(f32[64,5,64,128]{3,2,1,0:T(8,128)} %bitcast.35, f32[64,64,128]{2,1,0:T(8,128)} %bitcast.36, f32[5]{0:T(128)} %scale.1, f32[5]{0:T(128)} %ratio.1, s32[16,32]{1,0:T(8,128)} %bitcast.37, s32[16,32]{1,0:T(8,128)} %bitcast.38, s32[16,32]{1,0:T(8,128)} %bitcast.39, f32[16,32]{1,0:T(8,128)} %bitcast.40), custom_call_target="tpu_custom_call" | custom-call | tf_op jit(solution)/shard_map/overset_step/pallas_call | solution.py:508
  92.4 4.0 %write_out.1 = f32[64,5,64,128]{3,2,1,0:T(8,128)} custom-call(f32[5,64,64,128]{3,2,1,0:T(8,128)S(1)} %overset_step.1.result), custom_call_target="tpu_custom_call" | custom-call | tf_op jit(solution)/shard_map/write_out/pallas_call | solution.py:548

commit v4 on v3

--- a/solution.py
+++ b/solution.py
@@ -10,7 +10,7 @@
 MESH = pl.DeviceIdType.MESH
 STRIDE = 11
 UNROLL = 8
-TURN = 4
+TURN = 8
 
 
 def limited(first_diff, second_diff):
@@ -33,6 +33,7 @@
     filled,
     donors,
     tiles,
+    laid,
     ws,
     inverse,
     growth,
@@ -86,7 +87,7 @@
     def load(v):
         return pltpu.make_async_copy(flow.at[:, v], field.at[v], load_sem.at[v])
 
-    first_load = pltpu.make_async_copy(flow.at[:, 0], filled.at[pl.ds(0, width)], misc_sem.at[0])
+    first_load = pltpu.make_async_copy(flow.at[:, 0], filled.at[0, pl.ds(0, width)], misc_sem.at[0])
     first_load.start()
     speed_load = pltpu.make_async_copy(speed, ws.at[pl.ds(1, width)], misc_sem.at[1])
     speed_load.start()
@@ -120,13 +121,14 @@
         )
 
     def send_all(v, source):
-        def lay(x, carry):
-            for y in range(16):
+        def lay(outer, carry):
+            for k in range(16 * TURN):
+                x, y = outer * TURN + k // 16, k % 16
                 row = pl.ds((y // 8) * 8 * tiles_z + y % 8, tiles_z, stride=8)
-                tiles[x * 16 + y] = filled[x, row, :] if source is filled else source[v, x, row, :]
+                tiles[x * 16 + y] = filled[0, x, row, :] if source is filled else source[v, x, row, :]
             return carry
 
-        lax.fori_loop(0, width, lay, 0)
+        lax.fori_loop(0, width // TURN, lay, 0)
         if source is filled:
             pl.semaphore_wait(barrier, peers - 1 + streams - 1)
         for c in range(capacity):
@@ -222,7 +224,7 @@
 
     def factors(v):
         rate = scale[v]
-        slot = v % 2
+        half, slot = v % 2, v % 3
 
         def one(x, carry):
             new = []
@@ -230,14 +232,19 @@
                 prior = rate * ws[x, r, :]
                 here = rate * ws[x + 1, r, :]
                 inv = 100.0 / (1.0 + 100.0 * here)
-                inverse[x, r, :] = inv
+                inverse[half, x, r, :] = inv
                 grown = carry[i] * (prior * inv)
                 growth[slot, x, r, :] = grown
                 new.append(grown)
             return tuple(new)
 
+        def several(outer, carry):
+            for k in range(TURN):
+                carry = one(outer * TURN + k, carry)
+            return carry
+
         ones = tuple(jnp.ones((8, lanes), jnp.float32) for _ in tile_rows)
-        ended = lax.fori_loop(0, width, one, ones)
+        ended = lax.fori_loop(0, width // TURN, several, ones)
         for r, grown in zip(tile_rows, ended):
             last_growth[v, r, :] = grown
 
@@ -267,6 +274,8 @@
                 relay(v, kind, j).start()
 
     def fill(v):
+        turn = v % 2
+
         def take_peer(g, carry):
             for c in range(capacity):
                 donors[g * capacity + c] = arriving[v, g, pl.ds(c * tiles_z, tiles_z), :]
@@ -274,13 +283,11 @@
 
         lax.fori_loop(0, peers, take_peer, 0)
 
-        def scatter(x, carry):
-            for y in range(16):
+        def scatter(outer):
+            for k in range(16 * TURN):
+                x, y = outer * TURN + k // 16, k % 16
                 row = pl.ds((y // 8) * 8 * tiles_z + y % 8, tiles_z, stride=8)
-                filled[x, row, :] = donors[slot_of[y % 8, x * 2 + y // 8]]
-            return carry
-
-        lax.fori_loop(0, width, scatter, 0)
+                laid[x, row, :] = donors[slot_of[y % 8, x * 2 + y // 8]]
 
         def mix(outer, carry):
             first, before, last = carry
@@ -291,8 +298,8 @@
                 kept = []
                 for i in range(tiles_z):
                     r = tile_rows[half * tiles_z + i]
-                    value = rest * field[v, x, r, :] + w * filled[x, r, :]
-                    filled[x, r, :] = value
+                    value = rest * field[v, x, r, :] + w * laid[x, r, :]
+                    filled[turn, x, r, :] = value
                     kept.append(value)
                 i = outer * 2 * TURN + k
                 here = lane == i
@@ -301,14 +308,21 @@
                 last = jnp.where(here, pltpu.roll(kept[-1], (i + 1) % lanes, 1), last)
             return first, before, last
 
+        def both(outer, carry):
+            carry = mix(outer, carry)
+            scatter(outer + 1)
+            return carry
+
         zero = jnp.zeros((8, lanes), jnp.float32)
-        for i, value in enumerate(lax.fori_loop(0, width // TURN, mix, (zero, zero, zero))):
+        scatter(0)
+        edges = lax.fori_loop(0, width // TURN - 1, both, (zero, zero, zero))
+        for i, value in enumerate(mix(width // TURN - 1, edges)):
             packed[v, i] = value
 
     def halo_copy(v, kind):
         src, dst, target = (
-            (filled.at[pl.ds(width - 2, 2)], row_low.at[v], (b, s, (t + 1) % streams)),
-            (filled.at[0], row_high.at[v], (b, s, (t + streams - 1) % streams)),
+            (filled.at[v % 2, pl.ds(width - 2, 2)], row_low.at[v], (b, s, (t + 1) % streams)),
+            (filled.at[v % 2, 0], row_high.at[v], (b, s, (t + streams - 1) % streams)),
             (packed.at[v, pl.ds(1, 2)], col_low.at[v], (b, (s + 1) % spans, t)),
             (packed.at[v, 0], col_high.at[v], (b, (s + spans - 1) % spans, t)),
         )[kind]
@@ -332,6 +346,7 @@
                 act(halo_copy(v, kind))
 
     def sweep(v):
+        turn = v % 2
         rate = scale[v]
         rate_z = rate * ratio[v]
         is_first = lane == 0
@@ -339,7 +354,7 @@
         before2, before1, after1 = col_low[v, 0], col_low[v, 1], col_high[v]
         edge_face = before1 + 0.5 * limited(before1 - before2, packed[v, 0] - before1)
         for i, r in enumerate(tile_rows):
-            filled[width, r, :] = row_high[v, r, :]
+            filled[turn, width, r, :] = row_high[v, r, :]
 
         for half in range(2):
             mine = tile_rows[half * tiles_z : (half + 1) * tiles_z]
@@ -364,12 +379,12 @@
                     jnp.where(is_first, ([outside_face] + shifted)[i], shifted[i]) for i in n
                 ]
                 span_term = [rate_z * (behind[i] - face[i]) for i in n]
-                coming = [filled[x + 1, r, :] for r in mine]
+                coming = [filled[turn, x + 1, r, :] for r in mine]
                 next_diffs = [coming[i] - cells[i] for i in n]
                 face_x = [cells[i] + 0.5 * limited(diffs[i], next_diffs[i]) for i in n]
                 speed_x = [rate * ws[x + 1, r, :] for r in mine]
                 rest = [span_term[i] - speed_x[i] * face_x[i] for i in n]
-                update = [inverse[x, r, :] * (flux[i] + rest[i]) for i, r in enumerate(mine)]
+                update = [inverse[turn, x, r, :] * (flux[i] + rest[i]) for i, r in enumerate(mine)]
                 next_flux = [speed_x[i] * (update[i] + face_x[i]) for i in n]
                 for i, r in enumerate(mine):
                     field[v, x, r, :] = cells[i] + update[i]
@@ -382,7 +397,7 @@
                     carry = step(outer * UNROLL + k, carry, k == UNROLL - 1)
                 return carry
 
-            cells = [filled[0, r, :] for r in mine]
+            cells = [filled[turn, 0, r, :] for r in mine]
             up1 = [row_low[v, 1, r, :] for r in mine]
             up2 = [row_low[v, 0, r, :] for r in mine]
             diffs = [c - u for c, u in zip(cells, up1)]
@@ -394,7 +409,7 @@
             lax.fori_loop(0, width // UNROLL, steps, (cells, diffs, flux))
 
     def finish(v):
-        slot = v % 2
+        slot = v % 3
         for j in range(streams - 1):
 
             @pl.when(j < t)
@@ -411,12 +426,18 @@
                 for i, r in enumerate(tile_rows)
             ]
 
-        def one(x, carry):
-            for i, r in enumerate(tile_rows):
-                field[v, x, r, :] = field[v, x, r, :] + growth[slot, x, r, :] * inflow[i]
+        def one(outer, carry):
+            for k in range(TURN):
+                x = outer * TURN + k
+                new = [
+                    field[v, x, r, :] + growth[slot, x, r, :] * inflow[i]
+                    for i, r in enumerate(tile_rows)
+                ]
+                for r, value in zip(tile_rows, new):
+                    field[v, x, r, :] = value
             return carry
 
-        lax.fori_loop(0, width, one, 0)
+        lax.fori_loop(0, width // TURN, one, 0)
 
     def all_donors(v):
         return pltpu.make_async_remote_copy(
@@ -428,28 +449,41 @@
             device_id_type=MESH,
         )
 
-    def variable(v, carry):
-        factors(v)
-        relay_all(v, 1)
-        all_donors(v).wait_recv()
-        fill(v)
-        halos(v, sends, lambda copy: copy.start())
-
-        @pl.when(v + 2 < parts)
-        def _():
-            send_all(v + 2, field)
-
-        @pl.when(v > 0)
-        def _():
-            finish(v - 1)
-
+    def march(v):
         halos(v, receives, lambda copy: copy.wait_recv())
         sweep(v)
         relay_all(v, 0)
         halos(v, sends, lambda copy: copy.wait_send())
+
+    def variable(v, carry):
+        all_donors(v).wait_recv()
+        fill(v)
+        halos(v, sends, lambda copy: copy.start())
+
+        @pl.when(v + 2 < parts)
+        def _():
+            send_all(v + 2, field)
+
+        @pl.when(v > 0)
+        def _():
+            march(v - 1)
+
+        @pl.when(v + 1 < parts)
+        def _():
+            factors(v + 1)
+            relay_all(v + 1, 1)
+
+            @pl.when(v > 0)
+            def _():
+                finish(v - 1)
+
         return carry
 
+    factors(0)
+    relay_all(0, 1)
     lax.fori_loop(0, parts, variable, 0)
+    march(parts - 1)
+    finish(parts - 2)
     finish(parts - 1)
 
     for v in range(parts):
@@ -511,12 +545,13 @@
         in_specs=[anywhere, anywhere] + [scalars] * 6,
         out_specs=pl.BlockSpec(memory_space=pltpu.VMEM),
         scratch_shapes=[
-            vmem(width + 1, rows, 128),
+            vmem(2, width + 1, rows, 128),
             vmem(peers * capacity, tiles_z, 128),
             vmem(width * rows_y, tiles_z, 128),
+            vmem(width, rows, 128),
             vmem(width + 1, rows, 128),
-            vmem(width, rows, 128),
             vmem(2, width, rows, 128),
+            vmem(3, width, rows, 128),
             vmem(width, rows_y, 128),
             vmem(parts, peers, message, 128),
             vmem(parts, peers, message, 128),
@@ -541,7 +576,7 @@
             dma((5,)),
         ],
         compiler_params=pltpu.CompilerParams(
-            collective_id=1, has_side_effects=True, vmem_limit_bytes=44 * 1024 * 1024
+            collective_id=1, has_side_effects=True, vmem_limit_bytes=48 * 1024 * 1024
         ),
         name="overset_step",
     )(flow, speed, char_scale, span_ratio, *small)

time: 96.6 us -> 88.8 us (0.919)
  the two profiles are of different devices: /device:TPU:58 before, /device:TPU:24 now
where the time goes in v4:
time: 88.8 us; the launch traced here: 88.7 us
  Pallas kernels  88.7 us (100%)
    pallas_call x1, Pallas kernels, on_device(): pl.pallas_call(functools.partial(kernel, sizes), out_shape=pltpu.VMEM((pa...  84.6 us
    pallas_call x1, Pallas kernels, on_device(): pl.pallas_call(write_out, out_shape=jax.ShapeDtypeStruct(flow.shape, f32)...  4.01 us

profile of v4, /device:TPU:24, one launch (start us, length us, event | category | flops | bytes accessed | tf_op | source)
XLA Modules:
  0.0 88.7 jit_solution(6846304963807312130)
XLA Ops:
  0.0 84.6 %overset_step.1.result = f32[5,64,64,128]{3,2,1,0:T(8,128)S(1)} custom-call(f32[64,5,64,128]{3,2,1,0:T(8,128)} %bitcast.35, f32[64,64,128]{2,1,0:T(8,128)} %bitcast.36, f32[5]{0:T(128)} %scale.1, f32[5]{0:T(128)} %ratio.1, s32[16,32]{1,0:T(8,128)} %bitcast.37, s32[16,32]{1,0:T(8,128)} %bitcast.38, s32[16,32]{1,0:T(8,128)} %bitcast.39, f32[16,32]{1,0:T(8,128)} %bitcast.40), custom_call_target="tpu_custom_call" | custom-call | tf_op jit(solution)/shard_map/overset_step/pallas_call | solution.py:542
  84.7 4.0 %write_out.1 = f32[64,5,64,128]{3,2,1,0:T(8,128)} custom-call(f32[5,64,64,128]{3,2,1,0:T(8,128)S(1)} %overset_step.1.result), custom_call_target="tpu_custom_call" | custom-call | tf_op jit(solution)/shard_map/write_out/pallas_call | solution.py:583

commit v5 on v4

--- a/solution.py
+++ b/solution.py
@@ -90,9 +90,6 @@
     first_load = pltpu.make_async_copy(flow.at[:, 0], filled.at[0, pl.ds(0, width)], misc_sem.at[0])
     first_load.start()
     speed_load = pltpu.make_async_copy(speed, ws.at[pl.ds(1, width)], misc_sem.at[1])
-    speed_load.start()
-    for v in range(parts):
-        load(v).start()
 
     barrier = pltpu.get_barrier_semaphore()
 
@@ -145,6 +142,9 @@
         lax.fori_loop(1, peers, one, 0)
 
     first_load.wait()
+    speed_load.start()
+    for v in range(parts):
+        load(v).start()
     send_all(0, filled)
 
     speed_load.wait()
@@ -221,6 +221,7 @@
         speed_halo.wait_recv()
 
     tile_rows = [pl.ds(i * 8, 8) for i in range(rows // 8)]
+    half_rows = [pl.ds(i * (rows // 2), rows // 2) for i in range(2)]
 
     def factors(v):
         rate = scale[v]
@@ -249,11 +250,12 @@
             last_growth[v, r, :] = grown
 
     def relay(v, kind, j):
-        source = last_growth if kind else last_update
-        target = growth_in if kind else update_in
+        source = last_growth if kind == 2 else last_update
+        target = growth_in if kind == 2 else update_in
+        part = pl.ds(0, rows) if kind == 2 else half_rows[kind]
         return pltpu.make_async_remote_copy(
-            src_ref=source.at[v],
-            dst_ref=target.at[v, t],
+            src_ref=source.at[v, part],
+            dst_ref=target.at[v, t, part],
             send_sem=relay_send.at[v, kind, j],
             recv_sem=relay_recv.at[v, kind, t],
             device_id=at_stream((t + j) % streams),
@@ -261,9 +263,10 @@
         )
 
     def relay_from(v, kind, source):
-        target = growth_in if kind else update_in
+        target = growth_in if kind == 2 else update_in
+        part = pl.ds(0, rows) if kind == 2 else half_rows[kind]
         return pltpu.make_async_copy(
-            target.at[v, source], target.at[v, source], relay_recv.at[v, kind, source]
+            target.at[v, source, part], target.at[v, source, part], relay_recv.at[v, kind, source]
         )
 
     def relay_all(v, kind):
@@ -273,39 +276,40 @@
             def _():
                 relay(v, kind, j).start()
 
-    def fill(v):
+    def fill(v, half):
         turn = v % 2
+        group = 2 * TURN
+        mine = tile_rows[half * tiles_z : (half + 1) * tiles_z]
 
         def take_peer(g, carry):
             for c in range(capacity):
                 donors[g * capacity + c] = arriving[v, g, pl.ds(c * tiles_z, tiles_z), :]
             return carry
 
-        lax.fori_loop(0, peers, take_peer, 0)
+        if half == 0:
+            lax.fori_loop(0, peers, take_peer, 0)
 
         def scatter(outer):
-            for k in range(16 * TURN):
-                x, y = outer * TURN + k // 16, k % 16
-                row = pl.ds((y // 8) * 8 * tiles_z + y % 8, tiles_z, stride=8)
-                laid[x, row, :] = donors[slot_of[y % 8, x * 2 + y // 8]]
+            for k in range(8 * group):
+                x, y = outer * group + k // 8, k % 8
+                row = pl.ds(half * (rows // 2) + y, tiles_z, stride=8)
+                laid[x, row, :] = donors[slot_of[y, x * 2 + half]]
 
         def mix(outer, carry):
             first, before, last = carry
-            for k in range(2 * TURN):
-                x, half = outer * TURN + k // 2, k % 2
+            for k in range(group):
+                x = outer * group + k
                 w = blend[x, pl.ds(half * 8, 8), :]
                 rest = 1.0 - w
                 kept = []
-                for i in range(tiles_z):
-                    r = tile_rows[half * tiles_z + i]
+                for r in mine:
                     value = rest * field[v, x, r, :] + w * laid[x, r, :]
                     filled[turn, x, r, :] = value
                     kept.append(value)
-                i = outer * 2 * TURN + k
-                here = lane == i
-                first = jnp.where(here, pltpu.roll(kept[0], i, 1), first)
-                before = jnp.where(here, pltpu.roll(kept[-1], (i + 2) % lanes, 1), before)
-                last = jnp.where(here, pltpu.roll(kept[-1], (i + 1) % lanes, 1), last)
+                here = lane == x
+                first = jnp.where(here, pltpu.roll(kept[0], x, 1), first)
+                before = jnp.where(here, pltpu.roll(kept[-1], (x + 2) % lanes, 1), before)
+                last = jnp.where(here, pltpu.roll(kept[-1], (x + 1) % lanes, 1), last)
             return first, before, last
 
         def both(outer, carry):
@@ -315,22 +319,31 @@
 
         zero = jnp.zeros((8, lanes), jnp.float32)
         scatter(0)
-        edges = lax.fori_loop(0, width // TURN - 1, both, (zero, zero, zero))
-        for i, value in enumerate(mix(width // TURN - 1, edges)):
-            packed[v, i] = value
-
-    def halo_copy(v, kind):
+        edges = lax.fori_loop(0, width // group - 1, both, (zero, zero, zero))
+        for i, value in enumerate(mix(width // group - 1, edges)):
+            packed[v, half, i] = value
+
+    def halo_copy(v, half, kind):
+        part = half_rows[half]
         src, dst, target = (
-            (filled.at[v % 2, pl.ds(width - 2, 2)], row_low.at[v], (b, s, (t + 1) % streams)),
-            (filled.at[v % 2, 0], row_high.at[v], (b, s, (t + streams - 1) % streams)),
-            (packed.at[v, pl.ds(1, 2)], col_low.at[v], (b, (s + 1) % spans, t)),
-            (packed.at[v, 0], col_high.at[v], (b, (s + spans - 1) % spans, t)),
+            (
+                filled.at[v % 2, pl.ds(width - 2, 2), part],
+                row_low.at[v, pl.ds(0, 2), part],
+                (b, s, (t + 1) % streams),
+            ),
+            (
+                filled.at[v % 2, 0, part],
+                row_high.at[v, part],
+                (b, s, (t + streams - 1) % streams),
+            ),
+            (packed.at[v, half, pl.ds(1, 2)], col_low.at[v, half], (b, (s + 1) % spans, t)),
+            (packed.at[v, half, 0], col_high.at[v, half], (b, (s + spans - 1) % spans, t)),
         )[kind]
         return pltpu.make_async_remote_copy(
             src_ref=src,
             dst_ref=dst,
-            send_sem=halo_send.at[v, kind],
-            recv_sem=halo_recv.at[v, kind],
+            send_sem=halo_send.at[v, half, kind],
+            recv_sem=halo_recv.at[v, half, kind],
             device_id=target,
             device_id_type=MESH,
         )
@@ -338,92 +351,91 @@
     sends = (t < streams - 1, t > 0, s < spans - 1, s > 0)
     receives = (t > 0, t < streams - 1, s > 0, s < spans - 1)
 
-    def halos(v, which, act):
+    def halos(v, half, which, act):
         for kind in range(4):
 
             @pl.when(which[kind])
             def _():
-                act(halo_copy(v, kind))
-
-    def sweep(v):
+                act(halo_copy(v, half, kind))
+
+    def sweep(v, half):
         turn = v % 2
         rate = scale[v]
         rate_z = rate * ratio[v]
         is_first = lane == 0
         is_last = lane == lanes - 1
-        before2, before1, after1 = col_low[v, 0], col_low[v, 1], col_high[v]
-        edge_face = before1 + 0.5 * limited(before1 - before2, packed[v, 0] - before1)
-        for i, r in enumerate(tile_rows):
+        before2, before1, after1 = col_low[v, half, 0], col_low[v, half, 1], col_high[v, half]
+        edge_face = before1 + 0.5 * limited(before1 - before2, packed[v, half, 0] - before1)
+        mine = tile_rows[half * tiles_z : (half + 1) * tiles_z]
+        for r in mine:
             filled[turn, width, r, :] = row_high[v, r, :]
 
-        for half in range(2):
-            mine = tile_rows[half * tiles_z : (half + 1) * tiles_z]
-
-            def step(x, carry, end):
-                cells, diffs, flux = carry
-                n = range(tiles_z)
-                i = x * 2 + half
-                to_first = (lanes - i) % lanes
-                outside = pltpu.roll(before1, to_first, 1)
-                outside_face = pltpu.roll(edge_face, to_first, 1)
-                beyond = pltpu.roll(after1, lanes - 1 - i, 1)
-                right = [pltpu.roll(u, 1, 1) for u in cells]
-                left = [pltpu.roll(u, lanes - 1, 1) for u in cells]
-                low = [jnp.where(is_first, ([outside] + right)[i], right[i]) for i in n]
-                high = [jnp.where(is_last, (left + [beyond])[i + 1], left[i]) for i in n]
-                face = [
-                    cells[i] + 0.5 * limited(cells[i] - low[i], high[i] - cells[i]) for i in n
-                ]
-                shifted = [pltpu.roll(f, 1, 1) for f in face]
-                behind = [
-                    jnp.where(is_first, ([outside_face] + shifted)[i], shifted[i]) for i in n
-                ]
-                span_term = [rate_z * (behind[i] - face[i]) for i in n]
-                coming = [filled[turn, x + 1, r, :] for r in mine]
-                next_diffs = [coming[i] - cells[i] for i in n]
-                face_x = [cells[i] + 0.5 * limited(diffs[i], next_diffs[i]) for i in n]
-                speed_x = [rate * ws[x + 1, r, :] for r in mine]
-                rest = [span_term[i] - speed_x[i] * face_x[i] for i in n]
-                update = [inverse[turn, x, r, :] * (flux[i] + rest[i]) for i, r in enumerate(mine)]
-                next_flux = [speed_x[i] * (update[i] + face_x[i]) for i in n]
-                for i, r in enumerate(mine):
-                    field[v, x, r, :] = cells[i] + update[i]
-                    if end:
-                        last_update[v, r, :] = update[i]
-                return coming, next_diffs, next_flux
-
-            def steps(outer, carry):
-                for k in range(UNROLL):
-                    carry = step(outer * UNROLL + k, carry, k == UNROLL - 1)
-                return carry
-
-            cells = [filled[turn, 0, r, :] for r in mine]
-            up1 = [row_low[v, 1, r, :] for r in mine]
-            up2 = [row_low[v, 0, r, :] for r in mine]
-            diffs = [c - u for c, u in zip(cells, up1)]
-            flux = [
-                rate * ws[0, r, :] * (u + 0.5 * limited(u - u2, d))
-                for r, u, u2, d in zip(mine, up1, up2, diffs)
+        def step(x, carry, end):
+            cells, diffs, flux = carry
+            n = range(tiles_z)
+            to_first = (lanes - x) % lanes
+            outside = pltpu.roll(before1, to_first, 1)
+            outside_face = pltpu.roll(edge_face, to_first, 1)
+            beyond = pltpu.roll(after1, lanes - 1 - x, 1)
+            right = [pltpu.roll(u, 1, 1) for u in cells]
+            left = [pltpu.roll(u, lanes - 1, 1) for u in cells]
+            low = [jnp.where(is_first, ([outside] + right)[i], right[i]) for i in n]
+            high = [jnp.where(is_last, (left + [beyond])[i + 1], left[i]) for i in n]
+            face = [
+                cells[i] + 0.5 * limited(cells[i] - low[i], high[i] - cells[i]) for i in n
             ]
-
-            lax.fori_loop(0, width // UNROLL, steps, (cells, diffs, flux))
-
-    def finish(v):
+            shifted = [pltpu.roll(f, 1, 1) for f in face]
+            behind = [
+                jnp.where(is_first, ([outside_face] + shifted)[i], shifted[i]) for i in n
+            ]
+            span_term = [rate_z * (behind[i] - face[i]) for i in n]
+            coming = [filled[turn, x + 1, r, :] for r in mine]
+            next_diffs = [coming[i] - cells[i] for i in n]
+            face_x = [cells[i] + 0.5 * limited(diffs[i], next_diffs[i]) for i in n]
+            speed_x = [rate * ws[x + 1, r, :] for r in mine]
+            rest = [span_term[i] - speed_x[i] * face_x[i] for i in n]
+            update = [inverse[turn, x, r, :] * (flux[i] + rest[i]) for i, r in enumerate(mine)]
+            next_flux = [speed_x[i] * (update[i] + face_x[i]) for i in n]
+            for i, r in enumerate(mine):
+                field[v, x, r, :] = cells[i] + update[i]
+                if end:
+                    last_update[v, r, :] = update[i]
+            return coming, next_diffs, next_flux
+
+        def steps(outer, carry):
+            for k in range(UNROLL):
+                carry = step(outer * UNROLL + k, carry, k == UNROLL - 1)
+            return carry
+
+        cells = [filled[turn, 0, r, :] for r in mine]
+        up1 = [row_low[v, 1, r, :] for r in mine]
+        up2 = [row_low[v, 0, r, :] for r in mine]
+        diffs = [c - u for c, u in zip(cells, up1)]
+        flux = [
+            rate * ws[0, r, :] * (u + 0.5 * limited(u - u2, d))
+            for r, u, u2, d in zip(mine, up1, up2, diffs)
+        ]
+
+        lax.fori_loop(0, width // UNROLL, steps, (cells, diffs, flux))
+
+    def finish(v, half):
         slot = v % 3
+        mine = tile_rows[half * tiles_z : (half + 1) * tiles_z]
         for j in range(streams - 1):
 
             @pl.when(j < t)
             def _():
-                relay_from(v, 0, j).wait()
-                relay_from(v, 1, j).wait()
-
-        inflow = [jnp.zeros((8, lanes), jnp.float32) for _ in tile_rows]
+                relay_from(v, half, j).wait()
+                if half == 0:
+                    relay_from(v, 2, j).wait()
+
+        inflow = [jnp.zeros((8, lanes), jnp.float32) for _ in mine]
         for j in range(streams - 1):
             inflow = [
                 jnp.where(
                     j < t, growth_in[v, j, r, :] * inflow[i] + update_in[v, j, r, :], inflow[i]
                 )
-                for i, r in enumerate(tile_rows)
+                for i, r in enumerate(mine)
             ]
 
         def one(outer, carry):
@@ -431,9 +443,9 @@
                 x = outer * TURN + k
                 new = [
                     field[v, x, r, :] + growth[slot, x, r, :] * inflow[i]
-                    for i, r in enumerate(tile_rows)
+                    for i, r in enumerate(mine)
                 ]
-                for r, value in zip(tile_rows, new):
+                for r, value in zip(mine, new):
                     field[v, x, r, :] = value
             return carry
 
@@ -449,46 +461,43 @@
             device_id_type=MESH,
         )
 
-    def march(v):
-        halos(v, receives, lambda copy: copy.wait_recv())
-        sweep(v)
-        relay_all(v, 0)
-        halos(v, sends, lambda copy: copy.wait_send())
-
     def variable(v, carry):
         all_donors(v).wait_recv()
-        fill(v)
-        halos(v, sends, lambda copy: copy.start())
+        for half in range(2):
+            fill(v, half)
+            halos(v, half, sends, lambda copy: copy.start())
 
         @pl.when(v + 2 < parts)
         def _():
             send_all(v + 2, field)
 
-        @pl.when(v > 0)
-        def _():
-            march(v - 1)
-
         @pl.when(v + 1 < parts)
         def _():
             factors(v + 1)
-            relay_all(v + 1, 1)
-
-            @pl.when(v > 0)
-            def _():
-                finish(v - 1)
-
+            relay_all(v + 1, 2)
+
+        @pl.when(v > 0)
+        def _():
+            finish(v - 1, 0)
+            finish(v - 1, 1)
+
+        for half in range(2):
+            halos(v, half, receives, lambda copy: copy.wait_recv())
+            sweep(v, half)
+            relay_all(v, half)
+        for half in range(2):
+            halos(v, half, sends, lambda copy: copy.wait_send())
         return carry
 
     factors(0)
-    relay_all(0, 1)
+    relay_all(0, 2)
     lax.fori_loop(0, parts, variable, 0)
-    march(parts - 1)
-    finish(parts - 2)
-    finish(parts - 1)
+    for half in range(2):
+        finish(parts - 1, half)
 
     for v in range(parts):
         all_donors(v).wait_send()
-        for kind in range(2):
+        for kind in range(3):
             for j in range(1, streams):
 
                 @pl.when(t + j < streams)
@@ -555,11 +564,11 @@
             vmem(width, rows_y, 128),
             vmem(parts, peers, message, 128),
             vmem(parts, peers, message, 128),
-            vmem(parts, 3, 8, 128),
+            vmem(parts, 2, 3, 8, 128),
             vmem(parts, 2, rows, 128),
             vmem(parts, rows, 128),
+            vmem(parts, 2, 2, 8, 128),
             vmem(parts, 2, 8, 128),
-            vmem(parts, 8, 128),
             vmem(parts, rows, 128),
             vmem(parts, rows, 128),
             vmem(parts, streams, rows, 128),
@@ -569,10 +578,10 @@
             dma((parts,)),
             dma((parts,)),
             dma((parts,)),
-            dma((parts, 4)),
-            dma((parts, 4)),
-            dma((parts, 2, streams)),
-            dma((parts, 2, streams)),
+            dma((parts, 2, 4)),
+            dma((parts, 2, 4)),
+            dma((parts, 3, streams)),
+            dma((parts, 3, streams)),
             dma((5,)),
         ],
         compiler_params=pltpu.CompilerParams(

time: 88.8 us -> 90.5 us (1.019)
  the two profiles are of different devices: /device:TPU:24 before, /device:TPU:58 now
where the time goes in v5:
time: 90.5 us; the launch traced here: 89.6 us
  Pallas kernels  89.6 us (99%)
    pallas_call x1, Pallas kernels, on_device(): pl.pallas_call(functools.partial(kernel, sizes), out_shape=pltpu.VMEM((pa...  85.6 us
    pallas_call x1, Pallas kernels, on_device(): pl.pallas_call(write_out, out_shape=jax.ShapeDtypeStruct(flow.shape, f32)...  4.01 us

profile of v5, /device:TPU:58, one launch (start us, length us, event | category | flops | bytes accessed | tf_op | source)
XLA Modules:
  0.0 89.6 jit_solution(9381308816337809974)
XLA Ops:
  0.0 85.6 %overset_step.1.result = f32[5,64,64,128]{3,2,1,0:T(8,128)S(1)} custom-call(f32[64,5,64,128]{3,2,1,0:T(8,128)} %bitcast.35, f32[64,64,128]{2,1,0:T(8,128)} %bitcast.36, f32[5]{0:T(128)} %scale.1, f32[5]{0:T(128)} %ratio.1, s32[16,32]{1,0:T(8,128)} %bitcast.37, s32[16,32]{1,0:T(8,128)} %bitcast.38, s32[16,32]{1,0:T(8,128)} %bitcast.39, f32[16,32]{1,0:T(8,128)} %bitcast.40), custom_call_target="tpu_custom_call" | custom-call | tf_op jit(solution)/shard_map/overset_step/pallas_call | solution.py:551
  85.6 4.0 %write_out.1 = f32[64,5,64,128]{3,2,1,0:T(8,128)} custom-call(f32[5,64,64,128]{3,2,1,0:T(8,128)S(1)} %overset_step.1.result), custom_call_target="tpu_custom_call" | custom-call | tf_op jit(solution)/shard_map/write_out/pallas_call | solution.py:592

commit v6 on v4

--- a/solution.py
+++ b/solution.py
@@ -90,9 +90,6 @@
     first_load = pltpu.make_async_copy(flow.at[:, 0], filled.at[0, pl.ds(0, width)], misc_sem.at[0])
     first_load.start()
     speed_load = pltpu.make_async_copy(speed, ws.at[pl.ds(1, width)], misc_sem.at[1])
-    speed_load.start()
-    for v in range(parts):
-        load(v).start()
 
     barrier = pltpu.get_barrier_semaphore()
 
@@ -145,6 +142,9 @@
         lax.fori_loop(1, peers, one, 0)
 
     first_load.wait()
+    speed_load.start()
+    for v in range(parts):
+        load(v).start()
     send_all(0, filled)
 
     speed_load.wait()
@@ -460,13 +460,13 @@
         fill(v)
         halos(v, sends, lambda copy: copy.start())
 
+        @pl.when(v > 0)
+        def _():
+            march(v - 1)
+
         @pl.when(v + 2 < parts)
         def _():
             send_all(v + 2, field)
-
-        @pl.when(v > 0)
-        def _():
-            march(v - 1)
 
         @pl.when(v + 1 < parts)
         def _():

time: 88.8 us -> 89.2 us (level)
  no operation moved by 1% of the time
where the time goes in v6:
time: 89.2 us; the launch traced here: 89 us
  Pallas kernels  89 us (100%)
    pallas_call x1, Pallas kernels, on_device(): pl.pallas_call(functools.partial(kernel, sizes), out_shape=pltpu.VMEM((pa...  85 us
    pallas_call x1, Pallas kernels, on_device(): pl.pallas_call(write_out, out_shape=jax.ShapeDtypeStruct(flow.shape, f32)...  4.01 us

profile of v6, /device:TPU:24, one launch (start us, length us, event | category | flops | bytes accessed | tf_op | source)
XLA Modules:
  0.0 89.0 jit_solution(1858827783375934573)
XLA Ops:
  0.0 85.0 %overset_step.1.result = f32[5,64,64,128]{3,2,1,0:T(8,128)S(1)} custom-call(f32[64,5,64,128]{3,2,1,0:T(8,128)} %bitcast.35, f32[64,64,128]{2,1,0:T(8,128)} %bitcast.36, f32[5]{0:T(128)} %scale.1, f32[5]{0:T(128)} %ratio.1, s32[16,32]{1,0:T(8,128)} %bitcast.37, s32[16,32]{1,0:T(8,128)} %bitcast.38, s32[16,32]{1,0:T(8,128)} %bitcast.39, f32[16,32]{1,0:T(8,128)} %bitcast.40), custom_call_target="tpu_custom_call" | custom-call | tf_op jit(solution)/shard_map/overset_step/pallas_call | solution.py:542
  85.0 4.0 %write_out.1 = f32[64,5,64,128]{3,2,1,0:T(8,128)} custom-call(f32[5,64,64,128]{3,2,1,0:T(8,128)S(1)} %overset_step.1.result), custom_call_target="tpu_custom_call" | custom-call | tf_op jit(solution)/shard_map/write_out/pallas_call | solution.py:583
